TPU v7x, 32 devices: a whole 2x2x4 slice. The times are simulated.
32 devices in a mesh: row: 4 (over z), col: 2 (over y), rep: 4 (over x, core).
Axes of the slice: x: 2, y: 2, z: 4, core: 2. Of those that a mesh axis runs over, the one named last changes fastest.
Arguments:
- genotypes: bfloat16 [128, 16384], P(('row', 'col', 'rep')), may hold values from 0 to 2, as said below
Outputs:
- main_tiles: float32 [4, 2, 4096, 4096], P('row', 'col', 'rep')
- half_tiles: float32 [4, 4096, 4096], P('row', 'rep', 'col')
Inputs may be any that keep to these rules, and one draw needn't show every extreme that they name: `genotypes`: imputed dosages of the alternate allele, real-valued.
All inputs are finite; a program needn't handle non-finite values.
Results may differ from a plain program's by a relative error of at most 0.008.
Values may be sent and summed in bfloat16 or wider, within the bound.
A program may use at most 128 MiB of HBM per device.

v0:
```python
import jax
import jax.numpy as jnp
import numpy as np
from jax import lax
from jax.sharding import PartitionSpec as P


def body(genotypes):
    sample_rows, variants = genotypes.shape
    row_count = lax.axis_size("row")
    col_count = lax.axis_size("col")
    rep_count = lax.axis_size("rep")
    sample_count = sample_rows * row_count * col_count * rep_count
    block_width = variants // row_count
    slab_width = block_width // col_count
    pair_count = row_count * col_count
    blocked = genotypes.reshape(sample_rows, row_count, block_width)
    shift_table = np.array(
        [(brow + bcol) % row_count for brow in range(row_count) for bcol in range(col_count)],
        np.int32,
    )
    partner = jnp.take(blocked, shift_table, axis=1)
    slab_view = genotypes.reshape(sample_rows, pair_count, slab_width)
    far_slab = jnp.roll(slab_view, -(pair_count // 2), axis=1)
    own_block = jnp.broadcast_to(
        blocked[:, :, None, :], (sample_rows, row_count, col_count, block_width)
    )
    payload = jnp.concatenate(
        [partner, own_block.reshape(sample_rows, pair_count, block_width), far_slab], axis=2
    )
    payload_width = payload.shape[2]
    arrived = lax.all_to_all(payload, ("row", "col"), split_axis=1, concat_axis=0, tiled=True)
    arrived = arrived.reshape(-1, payload_width)
    values = arrived.astype(jnp.float32)
    col_dose, col_square = lax.psum(
        (jnp.sum(values, axis=0), jnp.sum(values * values, axis=0)), "rep"
    )
    col_mean = col_dose / sample_count
    col_spread = col_square / sample_count - col_mean * col_mean
    arrived = ((values - col_mean) * lax.rsqrt(col_spread + 1e-05)).astype(jnp.bfloat16)
    scale_factor = 1.0 / sample_count
    right_side = jnp.concatenate(
        [arrived[:, :block_width], arrived[:, payload_width - slab_width :]], axis=1
    )
    product = lax.dot_general(
        arrived[:, block_width : 2 * block_width],
        right_side,
        (((0,), (0,)), ((), ())),
        preferred_element_type=jnp.float32,
    )
    partial_value = product * scale_factor
    summed = lax.psum_scatter(
        partial_value.astype(jnp.bfloat16), "rep", scatter_dimension=0, tiled=True
    ).astype(jnp.float32)
    main_tile = summed[:, :block_width].reshape(1, 1, -1, block_width)
    half_tile = summed[:, block_width:].reshape(1, -1, slab_width)
    return (main_tile, half_tile)


def solution(mesh):
    placed = (P(("row", "col", "rep"), None),)
    return jax.shard_map(
        body,
        mesh=mesh,
        in_specs=placed,
        out_specs=(P("row", "col", "rep", None), P("row", "rep", "col")),
        check_vma=False,
    )
```

profile of v0, /device:TPU:0, one launch (start us, length us, event | category | flops | bytes accessed | tf_op | source)
XLA Modules:
  0.0 473.2 jit_solution(7252126721184291509)
XLA Ops:
  7.2 0.0 all-reduce.3.cloned.1.call-start
  7.2 0.7 pad_clamp_fusion
  7.9 0.9 fusion.6
  8.8 1.7 gather_fusion
  10.5 1.0 broadcast_in_dim.22
  11.5 0.3 maximum_maximum_fusion
  11.8 24.8 %all_to_all.4 = bf16[4,8,10240]{2,0,1:T(4,128)(2,1)S(1)} all-to-all(bf16[4,8,10240]{2,0,1:T(4,128)(2,1)S(1)} %maximum_maximum_fusion), channel_id=1, replica_groups=mesh['row'=4,'col'=2,'rep'=4] {'row','col'}, dimensions={1} | all-to-all | bytes 1310720 | tf_op jit(solution)/shard_map/all_to_all | solution.py:32
  36.6 1.3 convert_reduce_fusion
  37.8 0.0 all-reduce.3.cloned.1.call-update
  37.8 0.0 reduce-scatter.2.cloned.1.call-start
  37.9 0.1 convert_bitcast_fusion
  38.0 0.5 reshape.40
  38.5 28.0 %all-reduce.3.cloned.1.call-done = (f32[10240]{0:T(1024)}, f32[10240]{0:T(1024)}) async-done(((f32[10240]{0:T(1024)}, f32[10240]{0:T(1024)}), (f32[10240]{0:T(1024)}, f32[10240]{0:T(1024)})) %all-reduce.3.cloned.1.call-update) | async-done | bytes 81936 | tf_op jit(solution)/shard_map/psum | solution.py:35
  66.4 0.8 broadcast_multiply_fusion
  67.2 0.1 multiply_convert_fusion.1
  67.4 20.0 %multiply_convert_fusion = bf16[4096,6144]{1,0:T(8,128)(2,1)} fusion(bf16[32,2048]{1,0:T(8,128)(2,1)S(1)} %slice.36, bf16[32,4096]{1,0:T(8,128)(2,1)S(1)} %slice.35, bf16[32,10240]{1,0:T(8,128)(2,1)S(1)} %multiply_convert_fusion.1), kind=kOutput, calls=%fused_computation.1 | convolution fusion | flops 1661730816 | bytes 50987008 | tf_op jit(solution)/shard_map/dot_general | solution.py:45
  87.4 0.0 reduce-scatter.2.cloned.1.call-update
  87.4 344.9 %reduce-scatter.2.cloned.1.call-done = bf16[1024,6144]{1,0:T(8,128)(2,1)} async-done(((bf16[4096,6144]{1,0:T(8,128)(2,1)}), bf16[1024,6144]{1,0:T(8,128)(2,1)}) %reduce-scatter.2.cloned.1.call-update) | async-done | bytes 12582928 | tf_op jit(solution)/shard_map/reduce_scatter | solution.py:52
  432.3 14.4 %convert_element_type.34 = f32[1024,6144]{1,0:T(8,128)} convert(bf16[1024,6144]{1,0:T(8,128)(2,1)} %reduce-scatter.2.cloned.1.call-done) | non-fusion elementwise | flops 6291456 | bytes 37748736 | tf_op jit(solution)/shard_map/convert_element_type | solution.py:54
  446.8 7.9 %slice_bitcast_fusion.1 = f32[1,1024,2048]{2,1,0:T(8,128)} fusion(f32[1024,6144]{1,0:T(8,128)} %convert_element_type.34), kind=kLoop, calls=%fused_computation.3 | loop fusion | bytes 16777216 | tf_op jit(solution)/shard_map/reshape | solution.py:56
  454.7 11.7 %slice_bitcast_fusion = f32[1,1,1024,4096]{3,2,1,0:T(8,128)} fusion(f32[1024,6144]{1,0:T(8,128)} %convert_element_type.34), kind=kLoop, calls=%fused_computation.2 | loop fusion | bytes 33554432 | tf_op jit(solution)/shard_map/reshape | solution.py:55
  (2 shorter events, 0.0 us)
Async XLA Ops:
  7.2 59.3 %all-reduce.3.cloned.1.call-start = ((), (), s32[]{:S(2)}) async-start(), calls=%async_computation.3 | async-start | bytes 163840 | tf_op jit(solution)/shard_map/psum | solution.py:35
  37.8 394.5 %reduce-scatter.2.cloned.1.call-start = ((), (), s32[]{:S(2)}) async-start(), calls=%async_computation.2 | async-start | bytes 62914560 | tf_op jit(solution)/shard_map/reduce_scatter | solution.py:52
Sparse Core Ops, SparseCore 0:
  38.0 28.4 all-reduce.2
  87.5 344.7 reduce-scatter.1
where the time goes:
time: 474 us; the launch traced here: 473 us
  waiting for transfers between devices  373 us (79%)
  blocking collectives  24.8 us (5%)
  local copies, waits for them, and re-layouts  23.7 us (5%)
  matrix products  20 us (4%)
  other arithmetic  17.7 us (4%)
  between operations  14.1 us (3%)
    reduce_scatter x1, waiting for transfers between devices, body(): lax.psum_scatter(partial_value.astype(jnp.bfloat16), 'rep', scatter_dimen...  345 us
    psum x1, waiting for transfers between devices, body(): lax.psum((jnp.sum(values, axis=0), jnp.sum(values * values, axis=0)), 'rep')  28 us
    all_to_all x1, blocking collectives, body(): lax.all_to_all(payload, ('row', 'col'), split_axis=1, concat_axis=0, tile...  24.8 us
    dot_general x1, matrix products, body(): lax.dot_general(arrived[:, block_width:2 * block_width], right_side, (((0...  20 us
    convert_element_type x1, other arithmetic, body(): summed = lax.psum_scatter(partial_value.astype(jnp.bfloat16), 'rep', scat...  14.4 us
    reshape x1, local copies, waits for them, and re-layouts, body(): main_tile = summed[:, :block_width].reshape(1, 1, -1, block_width)  11.7 us
  transfers between devices with their start and end apart: 2, of which 2 were waited for; matrix products, arithmetic and copies ran while one was open for 0% of the time, Pallas kernels for 0%

commit v1 on v0

--- a/solution.py
+++ b/solution.py
@@ -1,8 +1,256 @@
+import functools
+
 import jax
 import jax.numpy as jnp
-import numpy as np
 from jax import lax
+from jax.experimental import pallas as pl
+from jax.experimental.pallas import tpu as pltpu
 from jax.sharding import PartitionSpec as P
+
+MESH = pl.DeviceIdType.MESH
+SUB = 4
+
+
+def gather_kernel(sizes, x_ref, out_ref, stage, zbuf, z_send, z_recv, p_send, p_recv, c_send, c_recv, l_sem):
+    rows, cols, reps = sizes
+    chips = reps // 2
+    r, c, q = lax.axis_index("row"), lax.axis_index("col"), lax.axis_index("rep")
+    chip, core = q // 2, q % 2
+    per_slab = reps // cols
+    six = reps + per_slab
+    w = stage.shape[-1]
+    unit = SUB * w
+
+    def plane(k):
+        return ((r + rows - k) % rows, c, q)
+
+    def peer(j):
+        c2 = (c + j // chips) % cols
+        chip2 = (chip + j % chips) % chips
+        return c2, chip2, (r, c2, chip2 * 2 + core)
+
+    partner = (r, c, chip * 2 + (1 - core))
+    barrier = pltpu.get_barrier_semaphore()
+    friends = [plane(k) for k in range(1, rows)] + [peer(j)[2] for j in range(1, cols * chips)] + [partner]
+    for friend in friends:
+        pl.semaphore_signal(barrier, inc=1, device_id=friend, device_id_type=MESH)
+
+    for u in range(rows * reps):
+        pieces = [x_ref[:, u * unit + j * w : u * unit + (j + 1) * w].astype(jnp.float32) for j in range(SUB)]
+        tile = jnp.concatenate(pieces, axis=0).astype(jnp.bfloat16)
+        stage[u] = tile
+        if u < reps:
+            stage[rows * reps + u] = tile
+
+    def plane_pieces(row):
+        far = ((row + rows // 2) % rows) * reps
+        return (
+            (far, 0, per_slab),
+            (row * reps, per_slab, 2 * reps),
+            (far + per_slab, per_slab + 2 * reps, per_slab),
+        )
+
+    for src, dst, count in plane_pieces(r):
+        for u in range(count):
+            zbuf[0, dst + u] = stage[src + u]
+    pl.semaphore_wait(barrier, len(friends))
+
+    def z_copies(k):
+        target = plane(k)
+        return [
+            pltpu.make_async_remote_copy(
+                src_ref=stage.at[pl.ds(src, count)],
+                dst_ref=zbuf.at[k, pl.ds(dst, count)],
+                send_sem=z_send.at[k, i],
+                recv_sem=z_recv.at[k, i],
+                device_id=target,
+                device_id_type=MESH,
+            )
+            for i, (src, dst, count) in enumerate(plane_pieces(target[0]))
+        ]
+
+    def p_copies(k, j):
+        c2, chip2, target = peer(j)
+        return [
+            pltpu.make_async_remote_copy(
+                src_ref=zbuf.at[k, pl.ds(src, count)],
+                dst_ref=out_ref.at[0, k, j, pl.ds(dst, count)],
+                send_sem=p_send.at[k, j, i],
+                recv_sem=p_recv.at[k, j, i],
+                device_id=target,
+                device_id_type=MESH,
+            )
+            for i, (src, dst, count) in enumerate(((six * c2, 0, six), (per_slab + 2 * chip2, six, 2)))
+        ]
+
+    def l_copies(k):
+        return [
+            pltpu.make_async_copy(
+                zbuf.at[k, pl.ds(src, count)], out_ref.at[0, k, 0, pl.ds(dst, count)], l_sem.at[k, i]
+            )
+            for i, (src, dst, count) in enumerate(((six * c, 0, six), (per_slab + 2 * chip, six, 2)))
+        ]
+
+    def c_copies(k):
+        return [
+            pltpu.make_async_remote_copy(
+                src_ref=out_ref.at[0, k, :, pl.ds(at, count)],
+                dst_ref=out_ref.at[1, k, :, pl.ds(at, count)],
+                send_sem=c_send.at[k, i],
+                recv_sem=c_recv.at[k, i],
+                device_id=partner,
+                device_id_type=MESH,
+            )
+            for i, (at, count) in enumerate(((0, six), (six, 2)))
+        ]
+
+    def spread(k):
+        for j in range(cols * chips - 1, 0, -1):
+            wide, narrow = p_copies(k, j)
+            wide.start()
+            pl.when(peer(j)[0] != 0)(narrow.start)
+        for copy in l_copies(k):
+            copy.start()
+
+    def share(k):
+        for copy in l_copies(k):
+            copy.wait()
+        for j in range(1, cols * chips):
+            wide, narrow = p_copies(k, j)
+            wide.wait_recv()
+            pl.when(c != 0)(narrow.wait_recv)
+        wide, narrow = c_copies(k)
+        wide.start()
+        pl.when(c != 0)(narrow.start)
+
+    order = [k for i in range(1, rows // 2 + 1) for k in ((i, rows - i) if 2 * i != rows else (i,))]
+    for k in order:
+        for copy in z_copies(k):
+            copy.start()
+    spread(0)
+    before = 0
+    for k in order:
+        for copy in z_copies(k):
+            copy.wait_recv()
+        spread(k)
+        share(before)
+        before = k
+    share(before)
+    for k in range(rows):
+        if k:
+            for copy in z_copies(k):
+                copy.wait_send()
+        for j in range(1, cols * chips):
+            wide, narrow = p_copies(k, j)
+            wide.wait_send()
+            pl.when(peer(j)[0] != 0)(narrow.wait_send)
+        wide, narrow = c_copies(k)
+        wide.wait()
+        pl.when(c != 0)(narrow.wait)
+
+
+def tile_kernel(sizes, samples, g_ref, main_ref, half_ref, left, right, main_buf, half_buf, sems):
+    rows, cols, reps = sizes
+    c, q = lax.axis_index("col"), lax.axis_index("rep")
+    per_slab = reps // cols
+    six = reps + per_slab
+    w = g_ref.shape[-1]
+    unit = SUB * w
+    pairs = g_ref.shape[0] // 2
+
+    def standardized(index, put):
+        low = lax.broadcasted_iota(jnp.int32, (pairs, 8, w), 1) < 4
+        for m in range(SUB // 2):
+            own = g_ref[:pairs, index, 8 * m : 8 * m + 8, :].astype(jnp.float32)
+            other = g_ref[pairs:, index, 8 * m : 8 * m + 8, :].astype(jnp.float32)
+            even = jnp.where(low, own, pltpu.roll(other, 4, 1))
+            odd = jnp.where(low, pltpu.roll(own, 4, 1), other)
+            for j, dosage in ((2 * m, even), (2 * m + 1, odd)):
+                dosage = dosage.reshape(8 * pairs, w)
+                average = jnp.sum(dosage, axis=0, keepdims=True) / samples
+                spread = jnp.sum(dosage * dosage, axis=0, keepdims=True) / samples - average * average
+                put(j, (dosage - average) * lax.rsqrt(spread + 1e-05))
+
+    def put_left(j, scaled):
+        left[j * w : (j + 1) * w, :] = scaled.T.astype(jnp.bfloat16)
+
+    standardized(jnp.where(c == 0, per_slab + q, six + q % 2), put_left)
+
+    copies = []
+    for u in range(six):
+        slot = u % 2
+        index = per_slab * (1 - c) + u if u < reps else reps * c + (u - reps)
+
+        def put_right(j, scaled):
+            right[slot, :, j * w : (j + 1) * w] = scaled.astype(jnp.bfloat16)
+
+        standardized(index, put_right)
+        buf, ref, at = (main_buf, main_ref.at[0, 0], u) if u < reps else (half_buf, half_ref.at[0], u - reps)
+        here = pl.ds(at * unit, unit)
+        step = unit // 2
+        for i in range(2):
+            band = pl.ds(i * step, step)
+            buf[band, here] = jnp.dot(
+                left[band, :], right[slot], preferred_element_type=jnp.float32
+            ) * (1.0 / samples)
+            copy = pltpu.make_async_copy(buf.at[band, here], ref.at[band, here], sems.at[u, i])
+            copy.start()
+            copies.append(copy)
+    for copy in copies:
+        copy.wait()
+
+
+def fast_body(sizes, genotypes):
+    rows, cols, reps = sizes
+    sample_rows, variants = genotypes.shape
+    samples = sample_rows * rows * cols * reps
+    unit = variants // (rows * reps)
+    w = unit // SUB
+    chips = reps // 2
+    per_slab = reps // cols
+    six = reps + per_slab
+    near = cols * chips
+    dma = pltpu.SemaphoreType.DMA
+    gathered = pl.pallas_call(
+        functools.partial(gather_kernel, sizes),
+        out_shape=jax.ShapeDtypeStruct((2, rows, near, six + 2, 16, w), jnp.bfloat16),
+        in_specs=[pl.BlockSpec(memory_space=pltpu.VMEM)],
+        out_specs=pl.BlockSpec(memory_space=pl.ANY),
+        scratch_shapes=[
+            pltpu.VMEM(((rows + 1) * reps, 16, w), jnp.bfloat16),
+            pltpu.VMEM((rows, 2 * six, 16, w), jnp.bfloat16),
+            dma((rows, 3)),
+            dma((rows, 3)),
+            dma((rows, near, 2)),
+            dma((rows, near, 2)),
+            dma((rows, 2)),
+            dma((rows, 2)),
+            dma((rows, 2)),
+        ],
+        compiler_params=pltpu.CompilerParams(collective_id=0, has_side_effects=True),
+        name="gather_samples",
+    )(genotypes)
+    gathered = gathered.reshape(2 * rows * near, six + 2, 16, w)
+    height = unit
+    wide, narrow = reps * unit, per_slab * unit
+    return pl.pallas_call(
+        functools.partial(tile_kernel, sizes, samples),
+        out_shape=(
+            jax.ShapeDtypeStruct((1, 1, height, wide), jnp.float32),
+            jax.ShapeDtypeStruct((1, height, narrow), jnp.float32),
+        ),
+        in_specs=[pl.BlockSpec(memory_space=pltpu.VMEM)],
+        out_specs=(pl.BlockSpec(memory_space=pl.ANY), pl.BlockSpec(memory_space=pl.ANY)),
+        scratch_shapes=[
+            pltpu.VMEM((height, samples), jnp.bfloat16),
+            pltpu.VMEM((2, samples, unit), jnp.bfloat16),
+            pltpu.VMEM((height, wide), jnp.float32),
+            pltpu.VMEM((height, narrow), jnp.float32),
+            dma((six, 2)),
+        ],
+        compiler_params=pltpu.CompilerParams(vmem_limit_bytes=48 * 1024 * 1024),
+        name="gram_tiles",
+    )(gathered)
 
 
 def body(genotypes):
@@ -15,11 +263,8 @@
     slab_width = block_width // col_count
     pair_count = row_count * col_count
     blocked = genotypes.reshape(sample_rows, row_count, block_width)
-    shift_table = np.array(
-        [(brow + bcol) % row_count for brow in range(row_count) for bcol in range(col_count)],
-        np.int32,
-    )
-    partner = jnp.take(blocked, shift_table, axis=1)
+    shifted = [jnp.roll(blocked, -bcol, axis=1) for bcol in range(col_count)]
+    partner = jnp.stack(shifted, axis=2).reshape(sample_rows, pair_count, block_width)
     slab_view = genotypes.reshape(sample_rows, pair_count, slab_width)
     far_slab = jnp.roll(slab_view, -(pair_count // 2), axis=1)
     own_block = jnp.broadcast_to(
@@ -58,9 +303,18 @@
 
 
 def solution(mesh):
+    sizes = (mesh.shape["row"], mesh.shape["col"], mesh.shape["rep"])
+
+    def local(genotypes):
+        unit = genotypes.shape[1] // (sizes[0] * sizes[2])
+        fits = sizes[1] == 2 and sizes[2] % 2 == 0 and sizes[0] % 2 == 0
+        if fits and genotypes.shape[0] == 4 and unit % (128 * SUB) == 0:
+            return fast_body(sizes, genotypes)
+        return body(genotypes)
+
     placed = (P(("row", "col", "rep"), None),)
     return jax.shard_map(
-        body,
+        local,
         mesh=mesh,
         in_specs=placed,
         out_specs=(P("row", "col", "rep", None), P("row", "rep", "col")),

time: 474 us -> 35 us (0.07)
  the two profiles are of different devices: /device:TPU:0 before, /device:TPU:9 now
where the time goes in v1:
time: 35 us; the launch traced here: 34.8 us
  Pallas kernels  32.6 us (93%)
  local copies, waits for them, and re-layouts  1.58 us (5%)
  between operations  0.65 us (2%)
    pallas_call x1, Pallas kernels, fast_body(): pl.pallas_call(functools.partial(gather_kernel, sizes), out_shape=jax.Sha...  23.4 us
    pallas_call x1, Pallas kernels, fast_body(): pl.pallas_call(functools.partial(tile_kernel, sizes, samples), out_shape=...  9.23 us
    unnamed x2, local copies, waits for them, and re-layouts  1.58 us

profile of v1, /device:TPU:9, one launch (start us, length us, event | category | flops | bytes accessed | tf_op | source)
XLA Modules:
  0.0 34.8 jit_solution(7898502572919050266)
XLA Ops:
  0.6 23.4 %gather_samples.1 = bf16[2,4,4,8,16,256]{5,4,3,2,1,0:T(8,128)(2,1)} custom-call(bf16[4,16384]{1,0:T(4,128)(2,1)} %x_ref.1), custom_call_target="tpu_custom_call" | custom-call | tf_op jit(solution)/shard_map/gather_samples/pallas_call | solution.py:214
  24.0 0.0 copy-start
  24.0 1.6 %copy-done = bf16[2,4,4,8,16,256]{5,4,3,2,1,0:T(8,128)(2,1)S(1)} copy-done((bf16[2,4,4,8,16,256]{5,4,3,2,1,0:T(8,128)(2,1)S(1)}, bf16[2,4,4,8,16,256]{5,4,3,2,1,0:T(8,128)(2,1)}, u32[]{:S(2)}) %copy-start) | copy-done | bytes 2097176
  25.6 9.2 %gram_tiles.1 = (f32[1,1,1024,4096]{3,2,1,0:T(8,128)}, f32[1,1024,2048]{2,1,0:T(8,128)}) custom-call(bf16[32,8,16,256]{3,2,1,0:T(8,128)(2,1)S(1)} %bitcast.1), custom_call_target="tpu_custom_call" | custom-call | tf_op jit(solution)/shard_map/gram_tiles/pallas_call | solution.py:236
Async XLA Ops:
  24.0 1.6 %copy-start = (bf16[2,4,4,8,16,256]{5,4,3,2,1,0:T(8,128)(2,1)S(1)}, bf16[2,4,4,8,16,256]{5,4,3,2,1,0:T(8,128)(2,1)}, u32[]{:S(2)}) copy-start(bf16[2,4,4,8,16,256]{5,4,3,2,1,0:T(8,128)(2,1)} %gather_samples.1) | copy-start | bytes 6291460

commit v2 on v1

--- a/solution.py
+++ b/solution.py
@@ -128,14 +128,12 @@
         for copy in z_copies(k):
             copy.start()
     spread(0)
-    before = 0
     for k in order:
         for copy in z_copies(k):
             copy.wait_recv()
         spread(k)
-        share(before)
-        before = k
-    share(before)
+    for k in [0] + order:
+        share(k)
     for k in range(rows):
         if k:
             for copy in z_copies(k):
@@ -227,7 +225,7 @@
             dma((rows, 2)),
             dma((rows, 2)),
         ],
-        compiler_params=pltpu.CompilerParams(collective_id=0, has_side_effects=True),
+        compiler_params=pltpu.CompilerParams(collective_id=0, has_side_effects=True, vmem_limit_bytes=4 * 1024 * 1024),
         name="gather_samples",
     )(genotypes)
     gathered = gathered.reshape(2 * rows * near, six + 2, 16, w)

time: 35 us -> 32 us (0.914)
  the two profiles are of different devices: /device:TPU:9 before, /device:TPU:0 now
where the time goes in v2:
time: 32 us; the launch traced here: 31.8 us
  Pallas kernels  30.3 us (95%)
  local copies, waits for them, and re-layouts  0.9 us (3%)
  between operations  0.65 us (2%)
    pallas_call x1, Pallas kernels, fast_body(): pl.pallas_call(functools.partial(gather_kernel, sizes), out_shape=jax.Sha...  21 us
    pallas_call x1, Pallas kernels, fast_body(): pl.pallas_call(functools.partial(tile_kernel, sizes, samples), out_shape=...  9.25 us
    unnamed x2, local copies, waits for them, and re-layouts  0.9 us

profile of v2, /device:TPU:0, one launch (start us, length us, event | category | flops | bytes accessed | tf_op | source)
XLA Modules:
  0.0 31.8 jit_solution(16829758820565969613)
XLA Ops:
  0.6 0.0 copy-start
  0.6 0.9 %copy-done = bf16[4,16384]{1,0:T(4,128)(2,1)S(1)} copy-done((bf16[4,16384]{1,0:T(4,128)(2,1)S(1)}, bf16[4,16384]{1,0:T(4,128)(2,1)}, u32[]{:S(2)}) %copy-start) | copy-done | bytes 131096
  1.5 21.0 %gather_samples.1 = bf16[2,4,4,8,16,256]{5,4,3,2,1,0:T(8,128)(2,1)S(1)} custom-call(bf16[4,16384]{1,0:T(4,128)(2,1)S(1)} %copy-done), custom_call_target="tpu_custom_call" | custom-call | tf_op jit(solution)/shard_map/gather_samples/pallas_call | solution.py:212
  22.6 9.2 %gram_tiles.1 = (f32[1,1,1024,4096]{3,2,1,0:T(8,128)}, f32[1,1024,2048]{2,1,0:T(8,128)}) custom-call(bf16[32,8,16,256]{3,2,1,0:T(8,128)(2,1)S(1)} %bitcast.1), custom_call_target="tpu_custom_call" | custom-call | tf_op jit(solution)/shard_map/gram_tiles/pallas_call | solution.py:234
Async XLA Ops:
  0.6 0.9 %copy-start = (bf16[4,16384]{1,0:T(4,128)(2,1)S(1)}, bf16[4,16384]{1,0:T(4,128)(2,1)}, u32[]{:S(2)}) copy-start(bf16[4,16384]{1,0:T(4,128)(2,1)} %x_ref.1) | copy-start | bytes 393220

commit v3 on v2

--- a/solution.py
+++ b/solution.py
@@ -185,8 +185,8 @@
         standardized(index, put_right)
         buf, ref, at = (main_buf, main_ref.at[0, 0], u) if u < reps else (half_buf, half_ref.at[0], u - reps)
         here = pl.ds(at * unit, unit)
-        step = unit // 2
-        for i in range(2):
+        step = unit // 4
+        for i in range(4):
             band = pl.ds(i * step, step)
             buf[band, here] = jnp.dot(
                 left[band, :], right[slot], preferred_element_type=jnp.float32
@@ -244,7 +244,7 @@
             pltpu.VMEM((2, samples, unit), jnp.bfloat16),
             pltpu.VMEM((height, wide), jnp.float32),
             pltpu.VMEM((height, narrow), jnp.float32),
-            dma((six, 2)),
+            dma((six, 4)),
         ],
         compiler_params=pltpu.CompilerParams(vmem_limit_bytes=48 * 1024 * 1024),
         name="gram_tiles",

time: 32 us -> 31.8 us (level)
  no operation moved by 1% of the time
where the time goes in v3:
time: 31.8 us; the launch traced here: 31.7 us
  Pallas kernels  30.2 us (95%)
  local copies, waits for them, and re-layouts  0.9 us (3%)
  between operations  0.65 us (2%)
    pallas_call x1, Pallas kernels, fast_body(): pl.pallas_call(functools.partial(gather_kernel, sizes), out_shape=jax.Sha...  21 us
    pallas_call x1, Pallas kernels, fast_body(): pl.pallas_call(functools.partial(tile_kernel, sizes, samples), out_shape=...  9.12 us
    unnamed x2, local copies, waits for them, and re-layouts  0.9 us

profile of v3, /device:TPU:0, one launch (start us, length us, event | category | flops | bytes accessed | tf_op | source)
XLA Modules:
  0.0 31.7 jit_solution(16870880181529025587)
XLA Ops:
  0.6 0.0 copy-start
  0.6 0.9 %copy-done = bf16[4,16384]{1,0:T(4,128)(2,1)S(1)} copy-done((bf16[4,16384]{1,0:T(4,128)(2,1)S(1)}, bf16[4,16384]{1,0:T(4,128)(2,1)}, u32[]{:S(2)}) %copy-start) | copy-done | bytes 131096
  1.5 21.0 %gather_samples.1 = bf16[2,4,4,8,16,256]{5,4,3,2,1,0:T(8,128)(2,1)S(1)} custom-call(bf16[4,16384]{1,0:T(4,128)(2,1)S(1)} %copy-done), custom_call_target="tpu_custom_call" | custom-call | tf_op jit(solution)/shard_map/gather_samples/pallas_call | solution.py:212
  22.6 9.1 %gram_tiles.1 = (f32[1,1,1024,4096]{3,2,1,0:T(8,128)}, f32[1,1024,2048]{2,1,0:T(8,128)}) custom-call(bf16[32,8,16,256]{3,2,1,0:T(8,128)(2,1)S(1)} %bitcast.1), custom_call_target="tpu_custom_call" | custom-call | tf_op jit(solution)/shard_map/gram_tiles/pallas_call | solution.py:234
Async XLA Ops:
  0.6 0.9 %copy-start = (bf16[4,16384]{1,0:T(4,128)(2,1)S(1)}, bf16[4,16384]{1,0:T(4,128)(2,1)}, u32[]{:S(2)}) copy-start(bf16[4,16384]{1,0:T(4,128)(2,1)} %x_ref.1) | copy-start | bytes 393220
